TPU v7x, 128 devices: a whole 4x4x4 slice. The times are simulated.
128 devices in a mesh: replica: 4 (over y), fsdp: 32 (over x, z, core).
Axes of the slice: x: 4, y: 4, z: 4, core: 2. Of those that a mesh axis runs over, the one named last changes fastest.
Arguments:
- global_params: float32 [1024, 28672], P(None, 'fsdp'), may hold values from -6 to 6
- local_params: float32 [4, 1024, 28672], P('replica', None, 'fsdp'), may hold values from -6 to 6
- flip_signs: int32 [28672], replicated, may hold values from 0 to 1
- momentum: float32 [1024, 28672], P('fsdp'), may hold values from -6 to 6
- stale_codes: float32 [1024, 28672], P('fsdp'), may hold values from -127 to 127
- stale_scale: float32 [1], replicated, may hold values from 2 to 12
Outputs:
- new_params: float32 [1024, 28672], P(None, 'fsdp')
- new_momentum: float32 [1024, 28672], P('fsdp')
- new_stale: float32 [1024, 28672], P('fsdp')
- new_scale: float32 [1], replicated
All inputs are finite; a program needn't handle non-finite values. Where the computation divides by a largest or mean magnitude, that divisor is 1e-20 or more.
Results may differ from a plain program's by a relative error of at most 0.00008.
Values sent between devices are 32-bit elements; how exact they have to be, the bound alone decides.
A program may use at most 192 MiB of HBM per device.

v0:
```python
import math

import jax
import jax.numpy as jnp
from jax import lax
from jax.sharding import PartitionSpec as P

BLOCK = 4096


def sylvester(order_size):
    indices = jnp.arange(order_size, dtype=jnp.int32)
    common_bits = indices[:, None] & indices[None, :]
    parity = jnp.zeros((order_size, order_size), jnp.int32)
    for bit_index in range(max(order_size.bit_length() - 1, 1)):
        parity = parity + (common_bits >> bit_index & 1)
    return jnp.where(parity % 2 == 0, 1.0, -1.0).astype(jnp.float32)


def rotate(row_block, block_len):
    small_order = block_len // 128
    left_table = sylvester(small_order)
    right_table = sylvester(128)
    row_total, width_total = row_block.shape
    pieces = row_block.reshape(row_total, width_total // block_len, small_order, 128)
    section_one = jnp.einsum("nkab,db->nkad", pieces, right_table, precision=lax.Precision.HIGHEST)
    section_two = jnp.einsum(
        "nkab,ca->nkcb", section_one, left_table, precision=lax.Precision.HIGHEST
    )
    return (section_two * (1.0 / math.sqrt(block_len))).reshape(row_total, width_total)


def body(global_params, local_params, flip_signs, momentum, stale_codes, stale_scale):
    shard_count = lax.axis_size("fsdp")
    worker_count = lax.axis_size("replica")
    row_count, col_count = global_params.shape
    flips = (2 * flip_signs - 1).astype(jnp.float32)
    pseudo_grad = (global_params - local_params[0]).reshape(
        shard_count, row_count // shard_count, col_count
    )
    rotated = rotate(
        lax.all_to_all(pseudo_grad, "fsdp", split_axis=0, concat_axis=2, tiled=True)[0] * flips,
        BLOCK,
    )[None][0]
    new_scale = lax.pmax(jnp.max(jnp.abs(rotated)), ("replica", "fsdp")) + 1e-06
    quant_codes = 127.0 * rotated / new_scale
    owned_sum = lax.psum_scatter(quant_codes, "replica", scatter_dimension=0, tiled=True)
    first_row = lax.axis_index("replica") * owned_sum.shape[0]
    owned_average = owned_sum / worker_count
    stale_rows = lax.dynamic_slice_in_dim(stale_codes, first_row, owned_sum.shape[0], 0)
    mixed = 0.5 * (new_scale / 127.0) * owned_average + 0.5 * (stale_scale[0] / 127.0) * stale_rows
    owned_grad = rotate(mixed, BLOCK) * flips
    outer_grad, new_stale = (
        lax.all_gather(owned_grad, "replica", axis=0, tiled=True),
        lax.all_gather(owned_average, "replica", axis=0, tiled=True),
    )
    new_momentum = 0.9 * momentum + outer_grad
    nesterov_step = outer_grad + 0.9 * new_momentum
    returned = lax.all_to_all(nesterov_step[None], "fsdp", split_axis=2, concat_axis=0, tiled=True)
    new_params = global_params - 0.7 * returned.reshape(row_count, col_count)
    return (new_params, new_momentum, new_stale, new_scale.reshape(1))


def solution(mesh):
    placed = (
        P(None, "fsdp"),
        P("replica", None, "fsdp"),
        P(),
        P("fsdp", None),
        P("fsdp", None),
        P(),
    )
    return jax.shard_map(
        body,
        mesh=mesh,
        in_specs=placed,
        out_specs=(P(None, "fsdp"), P("fsdp", None), P("fsdp", None), P()),
        check_vma=False,
    )
```

profile of v0, /device:TPU:1, one launch (start us, length us, event | category | flops | bytes accessed | tf_op | source)
XLA Modules:
  0.0 566.2 jit_solution(170821773170502929)
XLA Ops:
  7.2 5.4 bitcast_subtract_fusion.1
  12.5 0.0 copy-start.1
  12.5 9.6 %all-to-all-start = ((f32[32,32,896]{2,1,0:T(8,128)}), f32[32,32,896]{2,1,0:T(8,128)}, u32[]{:S(2)}, u32[]{:S(2)}) async-start(f32[32,32,896]{2,1,0:T(8,128)} %bitcast.55), calls=%async_computation | async-start | bytes 7340032 | tf_op jit(solution)/shard_map/all_to_all | solution.py:42
  22.1 0.0 reduce-scatter.2.cloned.1.call-start
  22.2 0.0 copy-done.1
  22.2 45.9 %all-to-all-done = f32[32,32,896]{2,1,0:T(8,128)} async-done(((f32[32,32,896]{2,1,0:T(8,128)}), f32[32,32,896]{2,1,0:T(8,128)}, u32[]{:S(2)}, u32[]{:S(2)}) %all-to-all-start) | async-done | bytes 3670048 | tf_op jit(solution)/shard_map/all_to_all | solution.py:42
  68.2 6.0 %copy.19 = f32[1,32,32,896]{3,2,1,0:T(8,128)} copy(f32[1,32,32,896]{3,1,2,0:T(8,128)} %bitcast.6) | data formatting | bytes 7340032 | tf_op jit(solution)/shard_map/all_to_all | solution.py:42
  74.2 4.6 squeeze.8
  78.7 5.2 fusion
  84.0 5.7 %abs_reduce_fusion = (f32[]{:T(128)}, f32[32,32,7,128]{3,0,2,1:T(8,128)}) fusion(f32[32,7,32,128]{3,2,1,0:T(8,128)S(1)} %fusion), kind=kOutput, calls=%fused_computation.6 | convolution fusion | flops 355102720 | bytes 7340036 | tf_op jit(solution)/shard_map/nkab,ca->nkcb/dot_general | solution.py:27
  89.7 64.9 %pmax.7 = f32[]{:T(128)} all-reduce(f32[]{:T(128)} %get-tuple-element.12), channel_id=1, replica_groups=mesh['replica'=4,'fsdp'=32] {'replica','fsdp'}, use_global_device_ids=true, to_apply=%region_1.2 | all-reduce | flops 1 | bytes 8 | tf_op jit(solution)/shard_map/pmax | solution.py:45
  155.3 2.5 multiply_divide_fusion
  157.8 4.0 copy.31
  161.7 0.0 reduce-scatter.2.cloned.1.call-update
  161.8 0.0 all-gather.3.cloned.1.call-start
  162.5 39.5 %reduce-scatter.2.cloned.1.call-done = f32[8,28672]{1,0:T(8,128)} async-done(((f32[32,28672]{1,0:T(8,128)}), f32[8,28672]{1,0:T(8,128)}) %reduce-scatter.2.cloned.1.call-update) | async-done | bytes 917520 | tf_op jit(solution)/shard_map/reduce_scatter | solution.py:47
  202.0 2.5 broadcast_multiply_fusion.1
  204.5 0.9 fusion.3
  205.4 0.9 convolution_multiply_fusion
  206.4 1.5 bitcast_multiply_fusion
  207.8 0.0 all-gather.3.cloned.1.call-update
  207.8 0.3 all-gather.5.cloned.1.call-start
  208.1 0.5 all-gather.5.cloned.1.call-update
  208.6 43.0 %all-gather.3.cloned.1.call-done = f32[32,28672]{1,0:T(8,128)} async-done(((f32[8,28672]{1,0:T(8,128)}), f32[32,28672]{1,0:T(8,128)}) %all-gather.3.cloned.1.call-update) | async-done | bytes 3670032 | tf_op jit(solution)/shard_map/all_gather | solution.py:54
  251.6 6.8 %add_bitcast_fusion = (f32[1,32,28672]{2,1,0:T(8,128)}, f32[32,28672]{1,0:T(8,128)}) fusion(f32[32,28672]{1,0:T(8,128)} %all-gather.3.cloned.1.call-done, f32[32,28672]{1,0:T(8,128)} %param.9), kind=kLoop, calls=%fused_computation.4 | loop fusion | flops 3670016 | bytes 14680064 | tf_op jit(solution)/shard_map/broadcast_in_dim | solution.py:59
  258.4 28.2 %copy.21 = f32[1,32,28672]{1,0,2:T(1,128)} copy(f32[1,32,28672]{2,1,0:T(8,128)} %get-tuple-element.8) | data formatting | bytes 7340032 | tf_op jit(solution)/shard_map/broadcast_in_dim | solution.py:59
  286.6 0.6 broadcast.187
  287.2 128.6 %reduce.2 = f32[28672,32]{1,0:T(8,128)} reduce(f32[28672,1,32]{2,1,0:T(1,128)} %bitcast.52, f32[]{:T(128)} %broadcast.187), dimensions={1}, to_apply=%bitcast.43.reduce_sub_computation | reduce | bytes 7340036
  415.9 13.1 %reshape.47 = f32[32,1,28672]{2,1,0:T(1,128)} reshape(f32[28672,32]{1,0:T(8,128)} %reduce.2) | data formatting | bytes 7340032
  429.0 7.7 %all-to-all-start.1 = ((f32[32,1,28672]{2,1,0:T(1,128)}), f32[32,1,28672]{2,1,0:T(1,128)}, u32[]{:S(2)}, u32[]{:S(2)}) async-start(f32[32,1,28672]{2,1,0:T(1,128)} %reshape.47), calls=%async_computation.2 | async-start | bytes 7340032 | tf_op jit(solution)/shard_map/all_to_all | solution.py:59
  436.7 0.0 all-gather.5.cloned.1.call-done
  436.8 45.9 %all-to-all-done.1 = f32[32,1,28672]{2,1,0:T(1,128)} async-done(((f32[32,1,28672]{2,1,0:T(1,128)}), f32[32,1,28672]{2,1,0:T(1,128)}, u32[]{:S(2)}, u32[]{:S(2)}) %all-to-all-start.1) | async-done | bytes 3670048 | tf_op jit(solution)/shard_map/all_to_all | solution.py:59
  482.7 12.9 %reduce.3 = f32[32,28672]{1,0:T(8,128)} reduce(f32[32,1,28672]{2,1,0:T(1,128)} %all-to-all-done.1, f32[]{:T(128)} %broadcast.187), dimensions={1}, to_apply=%all_to_all.21.reduce_sub_computation | reduce | bytes 7340036 | tf_op jit(solution)/shard_map/all_to_all | solution.py:59
  495.6 27.4 %reshape.48 = f32[28672,1,32]{2,1,0:T(1,128)} reshape(f32[32,28672]{1,0:T(8,128)} %reduce.3) | data formatting | bytes 7340032
  523.0 17.6 %broadcast_multiply_fusion = f32[1,32,28672]{1,0,2:T(1,128)} fusion(f32[28672,1,32]{2,1,0:T(1,128)} %reshape.48), kind=kLoop, calls=%fused_computation | loop fusion | flops 917504 | bytes 7340032 | tf_op jit(solution)/shard_map/mul | solution.py:60
  540.5 10.7 %copy.22 = f32[32,1,32,896]{3,2,0,1:T(8,128)} copy(f32[32,1,32,896]{2,3,0,1:T(8,128)} %bitcast.51) | data formatting | bytes 7340032 | tf_op jit(solution)/shard_map/mul | solution.py:60
  551.2 0.0 copy-start
  551.2 5.5 bitcast_subtract_fusion
  556.7 0.0 copy-done
  556.7 1.8 copy.34
  (1 shorter events, 0.0 us)
Async XLA Ops:
  12.5 9.7 %copy-start.1 = (s32[28672]{0:T(1024)S(1)}, s32[28672]{0:T(1024)}, u32[]{:S(2)}) copy-start(s32[28672]{0:T(1024)} %param.8) | copy-start | bytes 344068
  12.5 55.6 %all-to-all-start = ((f32[32,32,896]{2,1,0:T(8,128)}), f32[32,32,896]{2,1,0:T(8,128)}, u32[]{:S(2)}, u32[]{:S(2)}) async-start(f32[32,32,896]{2,1,0:T(8,128)} %bitcast.55), calls=%async_computation | async-start | bytes 7340032 | tf_op jit(solution)/shard_map/all_to_all | solution.py:42
  22.1 179.9 %reduce-scatter.2.cloned.1.call-start = ((), (), s32[]{:S(2)}) async-start(), calls=%async_computation.3 | async-start | bytes 4587520 | tf_op jit(solution)/shard_map/reduce_scatter | solution.py:47
  161.8 89.9 %all-gather.3.cloned.1.call-start = ((), (), s32[]{:S(2)}) async-start(), calls=%async_computation.4 | async-start | bytes 4587520 | tf_op jit(solution)/shard_map/all_gather | solution.py:54
  207.8 228.9 %all-gather.5.cloned.1.call-start = ((), (), s32[]{:S(2)}) async-start(), calls=%async_computation.5 | async-start | bytes 4587520 | tf_op jit(solution)/shard_map/all_gather | solution.py:55
  429.0 53.7 %all-to-all-start.1 = ((f32[32,1,28672]{2,1,0:T(1,128)}), f32[32,1,28672]{2,1,0:T(1,128)}, u32[]{:S(2)}, u32[]{:S(2)}) async-start(f32[32,1,28672]{2,1,0:T(1,128)} %reshape.47), calls=%async_computation.2 | async-start | bytes 7340032 | tf_op jit(solution)/shard_map/all_to_all | solution.py:59
  551.2 5.5 copy-start
Sparse Core Ops, SparseCore 0:
  161.9 40.0 reduce-scatter.1
  208.0 43.5 all-gather.2
  253.9 44.1 all-gather.4
where the time goes:
time: 569 us; the launch traced here: 566 us
  other arithmetic  183 us (32%)
  waiting for transfers between devices  175 us (31%)
  local copies, waits for them, and re-layouts  96.4 us (17%)
  blocking collectives  64.9 us (11%)
  starting transfers between devices  17.7 us (3%)
  between operations  16.3 us (3%)
  matrix products  12.8 us (2%)
    unnamed x1, other arithmetic  129 us
    pmax x1, blocking collectives, body(): new_scale = lax.pmax(jnp.max(jnp.abs(rotated)), ('replica', 'fsdp')) + 1e-06  64.9 us
    unnamed x9, local copies, waits for them, and re-layouts  46.9 us
    all_to_all x1, waiting for transfers between devices, body(): lax.all_to_all(nesterov_step[None], 'fsdp', split_axis=2, concat_axis=0,...  45.9 us
    all_to_all x1, waiting for transfers between devices, body(): lax.all_to_all(pseudo_grad, 'fsdp', split_axis=0, concat_axis=2, tiled=True)  45.9 us
    all_gather x1, waiting for transfers between devices, body(): lax.all_gather(owned_grad, 'replica', axis=0, tiled=True)  43 us
    reduce_scatter x1, waiting for transfers between devices, body(): lax.psum_scatter(quant_codes, 'replica', scatter_dimension=0, tiled=True)  39.5 us
    broadcast_in_dim x1, local copies, waits for them, and re-layouts, body(): nesterov_step[None]  28.2 us
  transfers between devices with their start and end apart: 5, of which 4 were waited for; matrix products, arithmetic and copies ran while one was open for 31% of the time, Pallas kernels for 0%

commit v1 on v0

v1 whole, which is shorter than its diff:
```python
import functools

import jax
import jax.numpy as jnp
from jax import lax
from jax.experimental import pallas as pl
from jax.experimental.pallas import tpu as pltpu
from jax.sharding import PartitionSpec as P

MESH = pl.DeviceIdType.MESH
F32 = jnp.float32
BF16 = jnp.bfloat16
NF = 32
NR = 4
COLS = 896
FULL = NF * COLS
BLOCK = 4096
NBLK = FULL // BLOCK
PARTS = ((512, 384), (0, 512))
HALF = (pl.ds(0, NF // 2), pl.ds(NF // 2, NF // 2))
ORDER = (4, 12, 1, 3, 5, 15, 7, 13, 8, 2, 9, 6, 11, 14, 10)
PACKED = [sum(v << (4 * i) for i, v in enumerate(ORDER[5 * k : 5 * k + 5])) for k in range(3)]


def fwht(value):
    width = value.shape[1]
    if width == 128:
        return [value]
    left, right = value[:, : width // 2], value[:, width // 2 :]
    return fwht(left + right) + fwht(left - right)


def kernel(
    glob_in, loc_in, flip_in, mom_in, stale_in, sscale_in,
    np_out, nm_out, ns_out, sc_out,
    glob, pg, flips, mom, stale, rot, xrow, npf, table,
    r1a, r1b, r2a, r2b, gqa, gqb, gra, grb, tsend, trecv, nsend, nrecv, mxs, mxr, mys, myr,
    ld_sem, st_sem, lc_sem,
    rs_s, rs_r, sc_s, sc_r, t_s, t_r, gq_s, gq_r, ga_s, ga_r, gb_s, gb_r, ret_s, ret_r, mx_s, mx_r, my_s, my_r,
):
    r, f = lax.axis_index("replica"), lax.axis_index("fsdp")
    fx, fz, fc = f // 8, lax.rem(f // 2, 4), lax.rem(f, 2)
    right, left, far = lax.rem(r + 1, 4), lax.rem(r + 3, 4), lax.rem(r + 2, 4)
    to_right, to_left = (right, f), (left, f)

    def remote(src, dst, ss, rs, dev):
        return pltpu.make_async_remote_copy(
            src_ref=src, dst_ref=dst, send_sem=ss, recv_sem=rs, device_id=dev, device_id_type=MESH
        )

    def lanes(index, width=COLS, off=0):
        return pl.ds(pl.multiple_of(index * COLS + off, 128), width)

    def peers(s, dc):
        word = jnp.where(s < 5, PACKED[0], jnp.where(s < 10, PACKED[1], PACKED[2]))
        code = lax.rem(word >> (4 * lax.rem(s, 5)), 16)
        dx, dz = code // 4, lax.rem(code, 4)
        core = lax.rem(fc + dc, 2)
        to = lax.rem(fx + dx, 4) * 8 + lax.rem(fz + dz, 4) * 2 + core
        frm = lax.rem(fx + 4 - dx, 4) * 8 + lax.rem(fz + 4 - dz, 4) * 2 + core
        return to, frm

    other = f + 1 - 2 * fc

    def each_peer(fn, lo=0, hi=15, core=True):
        def step(s, carry):
            for dc in (0, 1):
                to, frm = peers(s, dc)
                fn(to, frm, 2 * s + dc)
            return carry

        lax.fori_loop(lo, hi, step, 0)
        if core:
            fn(other, other, 30)

    def exchange(src, dst, ss, rs):
        def start(to, frm, i):
            remote(src(to), dst(f), ss.at[i], rs.at[i], (r, to)).start()

        def wait(to, frm, i):
            remote(src(to), dst(frm), ss.at[i], rs.at[i], (r, to)).wait_recv()

        def drain(to, frm, i):
            remote(src(to), dst(f), ss.at[i], rs.at[i], (r, to)).wait_send()

        return start, wait, drain

    order = (far, right, left, r)
    loads = []
    for i, c in enumerate(order):
        a = pltpu.make_async_copy(loc_in.at[:, c], pg.at[:, c], ld_sem.at[2 * i])
        b = pltpu.make_async_copy(glob_in.at[:, c], glob.at[:, c], ld_sem.at[2 * i + 1])
        a.start()
        b.start()
        loads.append((a, b))
    ld_stale = pltpu.make_async_copy(stale_in, stale, ld_sem.at[8])
    ld_mom = pltpu.make_async_copy(mom_in, mom, ld_sem.at[9])
    ld_stale.start()
    ld_mom.start()

    barrier = pltpu.get_barrier_semaphore()

    def greet(s, carry):
        pl.semaphore_signal(
            barrier, inc=1, device_id=(r, lax.rem(f + s, NF)), device_id_type=MESH
        )
        return carry

    lax.fori_loop(1, NF, greet, 0)
    for s in (1, 2, 3):
        pl.semaphore_signal(barrier, inc=1, device_id=(lax.rem(r + s, 4), f), device_id_type=MESH)

    for (a, b), c in zip(loads, order):
        a.wait()
        b.wait()

        def diff(t, carry, c=c):
            rows = pl.ds(4 * t, 4)
            pg[rows, c] = glob[rows, c] - pg[rows, c]
            return carry

        lax.fori_loop(0, NF // 4, diff, 0)
    pl.semaphore_wait(barrier, NF - 1 + NR - 1)

    r1 = ((r1a, r1b)[0], (r1a, r1b)[1])
    r2 = (r2a, r2b)
    gq = (gqa, gqb)
    gr = (gra, grb)

    def cols(p):
        return pl.ds(PARTS[p][0], PARTS[p][1])

    def rs_copies(p):
        lo, hi = HALF
        return (
            remote(pg.at[lo, far, :, cols(p)], r1[p].at[0], rs_s.at[p, 0], rs_r.at[p, 0], to_right),
            remote(pg.at[hi, far, :, cols(p)], r1[p].at[1], rs_s.at[p, 1], rs_r.at[p, 1], to_left),
            remote(pg.at[hi, right, :, cols(p)], r2[p].at[0, hi], rs_s.at[p, 2], rs_r.at[p, 2], to_right),
            remote(pg.at[lo, left, :, cols(p)], r2[p].at[1, lo], rs_s.at[p, 3], rs_r.at[p, 3], to_left),
            remote(r1[p].at[0], r2[p].at[0, lo], rs_s.at[p, 4], rs_r.at[p, 4], to_right),
            remote(r1[p].at[1], r2[p].at[1, hi], rs_s.at[p, 5], rs_r.at[p, 5], to_left),
        )

    rs = (rs_copies(0), rs_copies(1))

    def rs_first(p):
        for i in range(4):
            rs[p][i].start()

    def rs_second(p):
        for side, c, base in ((0, right, 0), (1, left, NF // 2)):
            rs[p][side].wait_recv()

            def add(t, carry, side=side, c=c, base=base):
                rows = pl.ds(4 * t, 4)
                r1[p][side, rows] = r1[p][side, rows] + pg[pl.ds(base + 4 * t, 4), c, :, cols(p)]
                return carry

            lax.fori_loop(0, NF // 8, add, 0)
            rs[p][4 + side].start()

    def rs_last(p):
        for i in range(2, 6):
            rs[p][i].wait_recv()

        def add(t, carry):
            rows = pl.ds(4 * t, 4)
            gq[p][rows] = pg[rows, r, :, cols(p)] + (r2[p][0, rows] + r2[p][1, rows])
            return carry

        lax.fori_loop(0, NF // 4, add, 0)

    rs_first(0)

    sc_start, sc_wait, sc_drain = exchange(
        lambda to: pg.at[to], lambda frm: xrow.at[:, :, lanes(frm)], sc_s, sc_r
    )
    each_peer(sc_start, 0, 5, True)
    for i in range(NR):
        xrow[i, :, lanes(f)] = pg[f, i]

    flips[...] = jnp.broadcast_to((2 * flip_in[...] - 1).astype(F32), (8, FULL))
    bits = lax.broadcasted_iota(jnp.int32, (256, 128), 0) & lax.broadcasted_iota(jnp.int32, (256, 128), 1)
    parity = jnp.zeros((256, 128), jnp.int32)
    for b in range(7):
        parity = parity ^ (bits >> b)
    table[...] = jnp.where((parity & 1) == 0, 1.0 / 64.0, -1.0 / 64.0).astype(F32).astype(BF16)

    def hadamard(value):
        x = jnp.concatenate(fwht(value), axis=0)
        high = x.astype(BF16)
        low = (x - high.astype(F32)).astype(BF16)
        return jnp.dot(
            jnp.concatenate([high, low], axis=1), table[...], preferred_element_type=F32
        )

    def to_rows(value):
        return jnp.concatenate([value[8 * a : 8 * a + 8] for a in range(32)], axis=1)

    def blk(k):
        return pl.ds(pl.multiple_of(k * BLOCK, BLOCK), BLOCK)

    coef = 0.5 * (sscale_in[0] / 127.0)
    ld_stale.wait()

    def stale_step(t, carry):
        i, k = t // NBLK, lax.rem(t, NBLK)
        stale[i, :, blk(k)] = to_rows(hadamard(stale[i, :, blk(k)])) * (flips[:, blk(k)] * coef)
        return carry

    lax.fori_loop(0, NR * NBLK, stale_step, 0)
    ld_mom.wait()
    off1, wid1 = PARTS[1]
    off0, wid0 = PARTS[0]

    def t_step(g, carry):
        tsend[g] = 1.9 * stale[r, :, lanes(g, wid1, off1)] + 0.81 * mom[r, :, lanes(g, wid1, off1)]
        return carry

    lax.fori_loop(0, NF, t_step, 0)
    t_start, t_wait, t_drain = exchange(
        lambda to: tsend.at[to], lambda frm: trecv.at[frm], t_s, t_r
    )
    each_peer(t_start)
    trecv[f] = tsend[f]

    rs_second(0)
    rs_first(1)

    def gq_ops(p):
        return exchange(
            lambda to: gq[p].at[to], lambda frm: gr[p].at[r, frm], gq_s.at[p], gq_r.at[p]
        )

    gq0, gq1 = gq_ops(0), gq_ops(1)

    def gather(ref, lo, hi, ss, sr):
        del lo, hi
        return (
            remote(ref(r, 0), ref(r, 0), ss.at[0], sr.at[0], to_right),
            remote(ref(r, 1), ref(r, 1), ss.at[1], sr.at[1], to_left),
            remote(ref(r, 1), ref(r, 1), ss.at[2], sr.at[2], to_right),
            remote(ref(r, 0), ref(r, 0), ss.at[3], sr.at[3], to_left),
            remote(ref(left, 0), ref(left, 0), ss.at[4], sr.at[4], to_right),
            remote(ref(right, 1), ref(right, 1), ss.at[5], sr.at[5], to_left),
        )

    ga = [
        gather(lambda c, h, p=p: gr[p].at[c, HALF[h]], 0, 0, ga_s.at[p], ga_r.at[p]) for p in (0, 1)
    ]
    gb = gather(lambda c, h: npf.at[HALF[h], c, :, cols(1)], 0, 0, gb_s, gb_r)

    def gather_start(g):
        for i in range(4):
            g[i].start()

    def gather_forward(g):
        for i in range(2):
            g[i].wait_recv()
            g[4 + i].start()

    rs_last(0)
    each_peer(gq0[0])
    gra[r, f] = gqa[f]
    each_peer(sc_start, 5, 10, False)

    rs_second(1)
    each_peer(gq0[1])
    gather_start(ga[0])

    rs_last(1)
    each_peer(gq1[0])
    grb[r, f] = gqb[f]
    each_peer(t_wait)

    def np_step(t, carry):
        rows = pl.ds(4 * t, 4)
        npf[rows, r, :, cols(1)] = glob[rows, r, :, cols(1)] - 0.7 * (trecv[rows] + 0.2375 * gqb[rows])
        return carry

    lax.fori_loop(0, NF // 4, np_step, 0)
    gather_start(gb)
    each_peer(sc_start, 10, 15, False)

    gather_forward(ga[0])
    each_peer(gq1[1])
    gather_start(ga[1])
    gather_forward(gb)

    for i in range(2, 6):
        ga[0][i].wait_recv()

    def n_step(t, carry):
        i, g = t // NF, lax.rem(t, NF)
        nsend[g, i] = (
            1.9 * (0.125 * gra[i, g] + stale[i, :, lanes(g, wid0, off0)])
            + 0.81 * mom[i, :, lanes(g, wid0, off0)]
        )
        return carry

    lax.fori_loop(0, NR * NF, n_step, 0)
    ret_start, ret_wait, ret_drain = exchange(
        lambda to: nsend.at[to], lambda frm: nrecv.at[frm], ret_s, ret_r
    )
    each_peer(ret_start)
    nrecv[f] = nsend[f]

    each_peer(sc_wait)

    def scale_step(t, top):
        i, k = t // NBLK, lax.rem(t, NBLK)
        y = jnp.abs(hadamard(xrow[i, :, blk(k)] * flips[:, blk(k)]))
        return jnp.maximum(top, jnp.max(y.reshape(32, 8, 128), axis=0))

    mxs[...] = lax.fori_loop(0, NR * NBLK, scale_step, jnp.zeros((8, 128), F32))
    mx_start, mx_wait, mx_drain = exchange(lambda to: mxs, lambda frm: mxr.at[frm], mx_s, mx_r)
    each_peer(mx_start)
    mxr[f] = mxs[...]

    gather_forward(ga[1])

    def rows_of(i):
        def mom_step(g, carry):
            for p, (off, wid) in enumerate(PARTS):
                at = lanes(g, wid, off)
                v = gr[p][i, g]
                mom[i, :, at] = 0.9 * mom[i, :, at] + (0.125 * v + stale[i, :, at])
                rot[i, :, at] = v * flips[:, at]
            return carry

        lax.fori_loop(0, NF, mom_step, 0)
        pltpu.make_async_copy(mom.at[i], nm_out.at[i], st_sem.at[i]).start()

        def rot_step(k, carry):
            rot[i, :, blk(k)] = to_rows(hadamard(rot[i, :, blk(k)]))
            return carry

        lax.fori_loop(0, NBLK, rot_step, 0)

    rows_of(r)

    each_peer(mx_wait)
    mys[...] = jnp.max(mxr[...], axis=0)

    def my_copy(s):
        return remote(
            mys, myr.at[s - 1], my_s.at[s - 1], my_r.at[s - 1], (lax.rem(r + s, 4), f)
        )

    for s in (1, 2, 3):
        my_copy(s).start()

    ga[1][3].wait_recv()
    rows_of(right)
    ga[1][2].wait_recv()
    rows_of(left)

    for s in (1, 2, 3):
        my_copy(s).wait_recv()
    top = jnp.maximum(jnp.max(myr[...], axis=0), mys[...])
    scale = jnp.max(top) + 1e-06
    sc_out[0] = scale
    factor = 31.75 / jnp.broadcast_to(scale, (8, 128))

    each_peer(ret_wait)

    def np0_step(t, carry):
        npf[t, :, :, cols(0)] = glob[t, :, :, cols(0)] - 0.7 * nrecv[t]
        return carry

    lax.fori_loop(0, NF, np0_step, 0)
    for i in range(2, 6):
        gb[i].wait_recv()
    st_np = pltpu.make_async_copy(npf, np_out, st_sem.at[8])
    st_np.start()

    def finish(i):
        def fin_step(t, carry):
            at = pl.ds(pl.multiple_of(t * COLS, 128), COLS)
            rot[i, :, at] = rot[i, :, at] * jnp.concatenate([factor] * 7, axis=1)
            return carry

        lax.fori_loop(0, NF, fin_step, 0)
        pltpu.make_async_copy(rot.at[i], ns_out.at[i], st_sem.at[4 + i]).start()

    finish(r)
    finish(right)
    finish(left)
    for i in (4, 5):
        ga[1][i].wait_recv()
    rows_of(far)
    finish(far)

    for p in (0, 1):
        for c in rs[p]:
            c.wait_send()
        for c in ga[p]:
            c.wait_send()
    for c in gb:
        c.wait_send()
    for d in (sc_drain, t_drain, gq0[2], gq1[2], ret_drain, mx_drain):
        each_peer(d)
    for s in (1, 2, 3):
        my_copy(s).wait_send()
    for i in range(NR):
        pltpu.make_async_copy(mom.at[i], nm_out.at[i], st_sem.at[i]).wait()
        pltpu.make_async_copy(rot.at[i], ns_out.at[i], st_sem.at[4 + i]).wait()
    st_np.wait()


def body(global_params, local_params, flip_signs, momentum, stale_codes, stale_scale):
    shape = jax.ShapeDtypeStruct
    hbm = pl.BlockSpec(memory_space=pl.ANY)
    vmem = pl.BlockSpec(memory_space=pltpu.VMEM)
    smem = pl.BlockSpec(memory_space=pltpu.SMEM)
    dma = pltpu.SemaphoreType.DMA
    w0, w1 = PARTS[0][1], PARTS[1][1]
    col4, row4 = (NF, NR, 8, COLS), (NR, 8, FULL)

    def buf(*dims):
        return pltpu.VMEM(dims, F32)

    new_params, new_momentum, new_stale, new_scale = pl.pallas_call(
        kernel,
        out_shape=(shape(col4, F32), shape(row4, F32), shape(row4, F32), shape((1,), F32)),
        in_specs=[hbm, hbm, vmem, hbm, hbm, smem],
        out_specs=(hbm, hbm, hbm, smem),
        scratch_shapes=[
            buf(*col4), buf(*col4), buf(8, FULL), buf(*row4), buf(*row4), buf(*row4), buf(*row4), buf(*col4),
            pltpu.VMEM((256, 128), BF16),
            buf(2, NF // 2, 8, w0), buf(2, NF // 2, 8, w1), buf(2, NF, 8, w0), buf(2, NF, 8, w1),
            buf(NF, 8, w0), buf(NF, 8, w1), buf(NR, NF, 8, w0), buf(NR, NF, 8, w1),
            buf(NF, 8, w1), buf(NF, 8, w1), buf(NF, NR, 8, w0), buf(NF, NR, 8, w0),
            buf(8, 128), buf(NF, 8, 128), buf(8, 128), buf(3, 8, 128),
            dma((10,)), dma((9,)), dma((1,)),
            dma((2, 6)), dma((2, 6)), dma((31,)), dma((31,)), dma((31,)), dma((31,)),
            dma((2, 31)), dma((2, 31)), dma((2, 6)), dma((2, 6)), dma((6,)), dma((6,)),
            dma((31,)), dma((31,)), dma((31,)), dma((31,)), dma((3,)), dma((3,)),
        ],
        compiler_params=pltpu.CompilerParams(
            collective_id=0, has_side_effects=True, vmem_limit_bytes=48 * 2**20
        ),
        name="outer_step",
    )(
        global_params.reshape(col4), local_params.reshape(col4), flip_signs.reshape(1, FULL),
        momentum.reshape(row4), stale_codes.reshape(row4), stale_scale,
    )
    return (
        new_params.reshape(NF * NR * 8, COLS),
        new_momentum.reshape(NR * 8, FULL),
        new_stale.reshape(NR * 8, FULL),
        new_scale,
    )


def solution(mesh):
    placed = (
        P(None, "fsdp"),
        P("replica", None, "fsdp"),
        P(),
        P("fsdp", None),
        P("fsdp", None),
        P(),
    )
    return jax.shard_map(
        body,
        mesh=mesh,
        in_specs=placed,
        out_specs=(P(None, "fsdp"), P("fsdp", None), P("fsdp", None), P()),
        check_vma=False,
    )
```

time: 569 us -> 129 us (0.23)
  other arithmetic: 183 us -> 0 us
  waiting for transfers between devices: 175 us -> 0 us
  Pallas kernels: 0 us -> 116 us
  local copies, waits for them, and re-layouts: 96.4 us -> 9.45 us
  blocking collectives: 64.9 us -> 0 us
  starting transfers between devices: 17.7 us -> 0 us
  between operations: 16.3 us -> 3.07 us
  matrix products: 12.8 us -> 0 us
    unnamed x1 -> x0, other arithmetic: 129 us -> none
    pallas_call x0 -> x1, Pallas kernels: none -> 116 us  [body(): pl.pallas_call(kernel, out_shape=(shape(col4, F32), shape(row4, F32), sha...]
    all_to_all x2 -> x0, waiting for transfers between devices: 91.9 us -> none  [the longest x1 45.9 us: body(): lax.all_to_all(nesterov_step[None], 'fsdp', split_axis=2, concat_axis=0,...]
    pmax x1 -> x0, blocking collectives: 64.9 us -> none  [body(): new_scale = lax.pmax(jnp.max(jnp.abs(rotated)), ('replica', 'fsdp')) + 1e-06]
    all_gather x2 -> x0, waiting for transfers between devices: 43 us -> none  [the longest x1 43 us: body(): lax.all_gather(owned_grad, 'replica', axis=0, tiled=True)]
    reduce_scatter x1 -> x0, waiting for transfers between devices: 39.5 us -> none  [body(): lax.psum_scatter(quant_codes, 'replica', scatter_dimension=0, tiled=True)]
    unnamed x9, local copies, waits for them, and re-layouts: 46.9 us -> 9.45 us
    broadcast_in_dim x1 -> x0, local copies, waits for them, and re-layouts: 28.2 us -> none  [body(): nesterov_step[None]]
  transfers between devices with their start and end apart: 5 -> 0, of which waited for: 4 -> 0; matrix products, arithmetic and copies ran while one was open for 31% -> 0% of each run, Pallas kernels for 0% -> 0%
where the time goes in v1:
time: 129 us; the launch traced here: 128 us
  Pallas kernels  116 us (90%)
  local copies, waits for them, and re-layouts  9.45 us (7%)
  between operations  3.07 us (2%)
    pallas_call x1, Pallas kernels, body(): pl.pallas_call(kernel, out_shape=(shape(col4, F32), shape(row4, F32), sha...  116 us
    unnamed x9, local copies, waits for them, and re-layouts  9.45 us

profile of v1, /device:TPU:1, one launch (start us, length us, event | category | flops | bytes accessed | tf_op | source)
XLA Modules:
  0.0 128.0 jit_solution(3336846965274710551)
XLA Ops:
  1.3 0.0 copy-start
  1.3 0.9 copy-done
  2.2 115.5 %outer_step.1 = (f32[32,4,8,896]{3,2,1,0:T(8,128)S(1)}, f32[4,8,28672]{2,1,0:T(8,128)}, f32[4,8,28672]{2,1,0:T(8,128)}, f32[1]{0:T(128)}) custom-call(f32[32,4,8,896]{3,2,1,0:T(8,128)} %bitcast.10, f32[32,4,8,896]{3,2,1,0:T(8,128)} %bitcast.11, s32[1,28672]{1,0:T(1,128)S(1)} %bitcast.9, f32[4,8,28672]{2,1,0:T(8,128)} %bitcast.12, f32[4,8,28672]{2,1,0:T(8,128)} %bitcast.13, ...), custom_call_target="tpu_custom_call" | custom-call | tf_op jit(solution)/shard_map/outer_step/pallas_call | solution.py:423
  117.7 0.0 copy-start.2
  117.7 1.9 %copy.15 = f32[1024,896]{1,0:T(8,128)} copy(f32[1024,896]{1,0:T(8,128)S(1)} %bitcast.8) | data formatting | bytes 7340032
  119.6 1.5 %copy-done.2 = f32[4,8,28672]{2,1,0:T(8,128)S(1)} copy-done((f32[4,8,28672]{2,1,0:T(8,128)S(1)}, f32[4,8,28672]{2,1,0:T(8,128)}, u32[]{:S(2)}) %copy-start.2) | copy-done | bytes 3670040
  121.1 0.0 copy-start.1
  121.1 1.9 %copy.16 = f32[32,28672]{1,0:T(8,128)} copy(f32[32,28672]{1,0:T(8,128)S(1)} %bitcast.15) | data formatting | bytes 7340032
  123.0 1.5 %copy-done.1 = f32[4,8,28672]{2,1,0:T(8,128)S(1)} copy-done((f32[4,8,28672]{2,1,0:T(8,128)S(1)}, f32[4,8,28672]{2,1,0:T(8,128)}, u32[]{:S(2)}) %copy-start.1) | copy-done | bytes 3670040
  124.4 1.8 %copy.17 = f32[32,28672]{1,0:T(8,128)} copy(f32[32,28672]{1,0:T(8,128)S(1)} %bitcast.14) | data formatting | bytes 7340032
Async XLA Ops:
  1.3 0.9 copy-start
  117.7 3.4 %copy-start.2 = (f32[4,8,28672]{2,1,0:T(8,128)S(1)}, f32[4,8,28672]{2,1,0:T(8,128)}, u32[]{:S(2)}) copy-start(f32[4,8,28672]{2,1,0:T(8,128)} %get-tuple-element.9) | copy-start | bytes 11010052
  121.1 3.4 %copy-start.1 = (f32[4,8,28672]{2,1,0:T(8,128)S(1)}, f32[4,8,28672]{2,1,0:T(8,128)}, u32[]{:S(2)}) copy-start(f32[4,8,28672]{2,1,0:T(8,128)} %get-tuple-element.10) | copy-start | bytes 11010052

commit v2 on v1

v2 whole, which is shorter than its diff:
```python
import jax
import jax.numpy as jnp
from jax import lax
from jax.experimental import pallas as pl
from jax.experimental.pallas import tpu as pltpu
from jax.sharding import PartitionSpec as P

MESH = pl.DeviceIdType.MESH
F32 = jnp.float32
BF16 = jnp.bfloat16
NF = 32
NR = 4
COLS = 896
FULL = NF * COLS
BLOCK = 4096
NBLK = FULL // BLOCK
PARTS = ((640, 256), (0, 640))
CUTS = (5, 10)
HALF = (pl.ds(0, NF // 2), pl.ds(NF // 2, NF // 2))
ORDER = (4, 12, 1, 3, 5, 15, 7, 13, 8, 2, 9, 6, 11, 14, 10)
PACKED = [sum(v << (4 * i) for i, v in enumerate(ORDER[5 * k : 5 * k + 5])) for k in range(3)]


def fwht(value):
    width = value.shape[1]
    if width == 128:
        return [value]
    left, right = value[:, : width // 2], value[:, width // 2 :]
    return fwht(left + right) + fwht(left - right)


def kernel(
    glob_in, loc_in, flip_in, mom_in, stale_in, sscale_in,
    npf, mom, rot, top_out,
    glob, pg, signs, flips, stale, xrow, table,
    r1a, r1b, r2a, r2b, gqa, gqb, gra, grb, tsend, trecv, nsend, nrecv, mxs, mxr, mys, myr,
    ld_sem,
    rs_s, rs_r, sc_s, sc_r, t_s, t_r, gq_s, gq_r, ga_s, ga_r, gb_s, gb_r, ret_s, ret_r, mx_s, mx_r, my_s, my_r,
):
    r, f = lax.axis_index("replica"), lax.axis_index("fsdp")
    fx, fz, fc = f // 8, lax.rem(f // 2, 4), lax.rem(f, 2)
    right, left, far = lax.rem(r + 1, 4), lax.rem(r + 3, 4), lax.rem(r + 2, 4)
    to_right, to_left = (right, f), (left, f)

    def remote(src, dst, ss, rs, dev):
        return pltpu.make_async_remote_copy(
            src_ref=src, dst_ref=dst, send_sem=ss, recv_sem=rs, device_id=dev, device_id_type=MESH
        )

    def lanes(index, width=COLS, off=0):
        return pl.ds(pl.multiple_of(index * COLS + off, 128), width)

    def peers(s, dc):
        word = jnp.where(s < 5, PACKED[0], jnp.where(s < 10, PACKED[1], PACKED[2]))
        code = lax.rem(word >> (4 * lax.rem(s, 5)), 16)
        dx, dz = code // 4, lax.rem(code, 4)
        core = lax.rem(fc + dc, 2)
        to = lax.rem(fx + dx, 4) * 8 + lax.rem(fz + dz, 4) * 2 + core
        frm = lax.rem(fx + 4 - dx, 4) * 8 + lax.rem(fz + 4 - dz, 4) * 2 + core
        return to, frm

    other = f + 1 - 2 * fc

    def each_peer(fn, lo=0, hi=15, core=True):
        def step(s, carry):
            for dc in (0, 1):
                to, frm = peers(s, dc)
                fn(to, frm, 2 * s + dc)
            return carry

        lax.fori_loop(lo, hi, step, 0)
        if core:
            fn(other, other, 30)

    def exchange(src, dst, ss, rs, all_src, all_dst):
        def start(to, frm, i):
            remote(src(to), dst(f), ss, rs, (r, to)).start()

        def wait():
            remote(all_src, all_dst, ss, rs, (r, other)).wait_recv()

        def drain():
            remote(all_src, all_dst, ss, rs, (r, other)).wait_send()

        return start, wait, drain

    most = pl.ds(0, NF - 1)

    order = (far, right, left, r)
    loads = []
    for i, c in enumerate(order):
        a = pltpu.make_async_copy(loc_in.at[:, c], pg.at[:, c], ld_sem.at[2 * i])
        b = pltpu.make_async_copy(glob_in.at[:, c], glob.at[:, c], ld_sem.at[2 * i + 1])
        a.start()
        b.start()
        loads.append((a, b))
    ld_stale = pltpu.make_async_copy(stale_in, stale, ld_sem.at[8])
    ld_mom = pltpu.make_async_copy(mom_in, mom, ld_sem.at[9])
    ld_signs = pltpu.make_async_copy(flip_in, signs, ld_sem.at[10])
    ld_signs.start()
    ld_stale.start()
    ld_mom.start()

    barrier = pltpu.get_barrier_semaphore()

    def greet(s, carry):
        pl.semaphore_signal(
            barrier, inc=1, device_id=(r, lax.rem(f + s, NF)), device_id_type=MESH
        )
        return carry

    lax.fori_loop(1, NF, greet, 0)
    for s in (1, 2, 3):
        pl.semaphore_signal(barrier, inc=1, device_id=(lax.rem(r + s, 4), f), device_id_type=MESH)

    def difference(i):
        c = order[i]
        for load in loads[i]:
            load.wait()

        def diff(t, carry):
            rows = pl.ds(4 * t, 4)
            pg[rows, c] = glob[rows, c] - pg[rows, c]
            return carry

        lax.fori_loop(0, NF // 4, diff, 0, unroll=2)

    difference(0)
    pl.semaphore_wait(barrier, NF - 1 + NR - 1)

    r1 = (r1a, r1b)
    r2 = (r2a, r2b)
    gq = (gqa, gqb)
    gr = (gra, grb)

    def cols(p):
        return pl.ds(PARTS[p][0], PARTS[p][1])

    def rs_copies(p):
        lo, hi = HALF
        return (
            remote(pg.at[lo, far, :, cols(p)], r1[p].at[0], rs_s.at[p, 0], rs_r.at[p, 0], to_right),
            remote(pg.at[hi, far, :, cols(p)], r1[p].at[1], rs_s.at[p, 1], rs_r.at[p, 1], to_left),
            remote(pg.at[hi, right, :, cols(p)], r2[p].at[0, hi], rs_s.at[p, 2], rs_r.at[p, 2], to_right),
            remote(pg.at[lo, left, :, cols(p)], r2[p].at[1, lo], rs_s.at[p, 3], rs_r.at[p, 3], to_left),
            remote(r1[p].at[0], r2[p].at[0, lo], rs_s.at[p, 4], rs_r.at[p, 4], to_right),
            remote(r1[p].at[1], r2[p].at[1, hi], rs_s.at[p, 5], rs_r.at[p, 5], to_left),
        )

    rs = (rs_copies(0), rs_copies(1))

    def rs_second(p):
        for side, c, base in ((0, right, 0), (1, left, NF // 2)):
            rs[p][side].wait_recv()

            def add(t, carry, side=side, c=c, base=base):
                rows = pl.ds(4 * t, 4)
                r1[p][side, rows] = r1[p][side, rows] + pg[pl.ds(base + 4 * t, 4), c, :, cols(p)]
                return carry

            lax.fori_loop(0, NF // 8, add, 0, unroll=2)
            rs[p][4 + side].start()

    def rs_last(p):
        for i in range(2, 6):
            rs[p][i].wait_recv()

        def add(t, carry):
            rows = pl.ds(4 * t, 4)
            gq[p][rows] = pg[rows, r, :, cols(p)] + (r2[p][0, rows] + r2[p][1, rows])
            return carry

        lax.fori_loop(0, NF // 4, add, 0, unroll=2)

    for i in (0, 1):
        rs[0][i].start()
    difference(1)
    difference(2)
    for i in (2, 3):
        rs[0][i].start()
    for i in (0, 1):
        rs[1][i].start()
    difference(3)

    sc_start, sc_wait, sc_drain = exchange(
        lambda to: pg.at[to], lambda frm: xrow.at[:, :, lanes(frm)], sc_s.at[0], sc_r.at[0],
        pg.at[most], xrow.at[:, :, pl.ds(0, (NF - 1) * COLS)],
    )
    each_peer(sc_start, 0, CUTS[0], True)
    for i in range(NR):
        xrow[i, :, lanes(f)] = pg[f, i]

    rs_second(0)
    for i in (2, 3):
        rs[1][i].start()

    ld_signs.wait()

    def flip_step(t, carry):
        rows = (2 * signs[pl.ds(8 * t, 8), :] - 1).astype(F32)
        flips[:, pl.ds(pl.multiple_of(t * 1024, 1024), 1024)] = jnp.concatenate(
            [jnp.broadcast_to(rows[i : i + 1], (8, 128)) for i in range(8)], axis=1
        )
        return carry

    lax.fori_loop(0, FULL // 1024, flip_step, 0, unroll=2)
    bits = lax.broadcasted_iota(jnp.int32, (256, 128), 0) & lax.broadcasted_iota(jnp.int32, (256, 128), 1)
    parity = jnp.zeros((256, 128), jnp.int32)
    for b in range(7):
        parity = parity ^ (bits >> b)
    table[...] = jnp.where((parity & 1) == 0, 1.0 / 64.0, -1.0 / 64.0).astype(F32).astype(BF16)

    def hadamard(value):
        x = jnp.concatenate(fwht(value), axis=0)
        high = x.astype(BF16)
        low = (x - high.astype(F32)).astype(BF16)
        return jnp.dot(
            jnp.concatenate([high, low], axis=1), table[...], preferred_element_type=F32
        )

    def to_rows(value):
        return jnp.concatenate([value[8 * a : 8 * a + 8] for a in range(32)], axis=1)

    def blk(k):
        return pl.ds(pl.multiple_of(k * BLOCK, BLOCK), BLOCK)

    coef = 0.5 * (sscale_in[0] / 127.0)
    ld_stale.wait()

    def stale_step(t, carry):
        i, k = t // NBLK, lax.rem(t, NBLK)
        stale[i, :, blk(k)] = to_rows(hadamard(stale[i, :, blk(k)])) * (flips[:, blk(k)] * coef)
        return carry

    lax.fori_loop(0, NR * NBLK, stale_step, 0, unroll=4)
    ld_mom.wait()
    off1, wid1 = PARTS[1]
    off0, wid0 = PARTS[0]

    def t_step(g, carry):
        tsend[g] = 1.9 * stale[r, :, lanes(g, wid1, off1)] + 0.81 * mom[r, :, lanes(g, wid1, off1)]
        return carry

    lax.fori_loop(0, NF, t_step, 0, unroll=4)
    t_start, t_wait, t_drain = exchange(
        lambda to: tsend.at[to], lambda frm: trecv.at[frm], t_s.at[0], t_r.at[0],
        tsend.at[most], trecv.at[most],
    )
    each_peer(t_start)
    trecv[f] = tsend[f]

    def gq_ops(p):
        return exchange(
            lambda to: gq[p].at[to], lambda frm: gr[p].at[r, frm], gq_s.at[p], gq_r.at[p],
            gq[p].at[most], gr[p].at[r, most],
        )

    gq0, gq1 = gq_ops(0), gq_ops(1)

    def gather(ref, ss, sr):
        return (
            remote(ref(r, 0), ref(r, 0), ss.at[0], sr.at[0], to_right),
            remote(ref(r, 1), ref(r, 1), ss.at[1], sr.at[1], to_left),
            remote(ref(r, 1), ref(r, 1), ss.at[2], sr.at[2], to_right),
            remote(ref(r, 0), ref(r, 0), ss.at[3], sr.at[3], to_left),
            remote(ref(left, 0), ref(left, 0), ss.at[4], sr.at[4], to_right),
            remote(ref(right, 1), ref(right, 1), ss.at[5], sr.at[5], to_left),
        )

    ga = [
        gather(lambda c, h, p=p: gr[p].at[c, HALF[h]], ga_s.at[p], ga_r.at[p]) for p in (0, 1)
    ]
    gb = gather(lambda c, h: npf.at[HALF[h], c, :, cols(1)], gb_s, gb_r)

    def gather_start(g):
        for i in range(4):
            g[i].start()

    def gather_forward(g):
        for i in range(2):
            g[i].wait_recv()
            g[4 + i].start()

    def rows_of(i):
        def mom_step(g, carry):
            for p, (off, wid) in enumerate(PARTS):
                at = lanes(g, wid, off)
                v = gr[p][i, g]
                mom[i, :, at] = 0.9 * mom[i, :, at] + (0.125 * v + stale[i, :, at])
                rot[i, :, at] = v * flips[:, at]
            return carry

        lax.fori_loop(0, NF, mom_step, 0, unroll=4)

        def rot_step(k, carry):
            rot[i, :, blk(k)] = to_rows(hadamard(rot[i, :, blk(k)]))
            return carry

        lax.fori_loop(0, NBLK, rot_step, 0, unroll=NBLK)

    rs_last(0)
    each_peer(gq0[0])
    gra[r, f] = gqa[f]
    each_peer(sc_start, CUTS[0], CUTS[1], False)
    rs_second(1)
    gq0[1]()
    gather_start(ga[0])

    rs_last(1)
    each_peer(gq1[0])
    each_peer(sc_start, CUTS[1], 15, False)
    grb[r, f] = gqb[f]
    t_wait()

    def np_step(t, carry):
        rows = pl.ds(4 * t, 4)
        npf[rows, r, :, cols(1)] = glob[rows, r, :, cols(1)] - 0.7 * (trecv[rows] + 0.2375 * gqb[rows])
        return carry

    lax.fori_loop(0, NF // 4, np_step, 0, unroll=2)
    gather_start(gb)
    gather_forward(ga[0])
    gq1[1]()
    gather_start(ga[1])

    for i in range(2, 6):
        ga[0][i].wait_recv()

    def n_step(t, carry):
        i, g = t // NF, lax.rem(t, NF)
        nsend[g, i] = (
            1.9 * (0.125 * gra[i, g] + stale[i, :, lanes(g, wid0, off0)])
            + 0.81 * mom[i, :, lanes(g, wid0, off0)]
        )
        return carry

    lax.fori_loop(0, NR * NF, n_step, 0, unroll=4)
    ret_start, ret_wait, ret_drain = exchange(
        lambda to: nsend.at[to], lambda frm: nrecv.at[frm], ret_s.at[0], ret_r.at[0],
        nsend.at[most], nrecv.at[most],
    )
    each_peer(ret_start)
    nrecv[f] = nsend[f]

    rows_of(r)
    gather_forward(ga[1])
    gather_forward(gb)

    sc_wait()

    def scale_step(t, top):
        i, k = t // NBLK, lax.rem(t, NBLK)
        y = jnp.abs(hadamard(xrow[i, :, blk(k)] * flips[:, blk(k)]))
        return jnp.maximum(top, jnp.max(y.reshape(32, 8, 128), axis=0))

    mxs[...] = lax.fori_loop(0, NR * NBLK, scale_step, jnp.zeros((8, 128), F32), unroll=4)
    mx_start, mx_wait, mx_drain = exchange(
        lambda to: mxs, lambda frm: mxr.at[frm], mx_s.at[0], mx_r.at[0], mxr.at[most], mxr.at[most]
    )
    each_peer(mx_start)
    mxr[f] = mxs[...]

    ga[1][3].wait_recv()
    rows_of(right)
    ga[1][2].wait_recv()
    rows_of(left)
    for i in (4, 5):
        ga[1][i].wait_recv()
    rows_of(far)

    mx_wait()
    mys[...] = jnp.max(mxr[...], axis=0)

    def my_copy(s):
        return remote(
            mys, myr.at[s - 1], my_s.at[s - 1], my_r.at[s - 1], (lax.rem(r + s, 4), f)
        )

    for s in (1, 2, 3):
        my_copy(s).start()

    ret_wait()

    def np0_step(t, carry):
        npf[t, :, :, cols(0)] = glob[t, :, :, cols(0)] - 0.7 * nrecv[t]
        return carry

    lax.fori_loop(0, NF, np0_step, 0, unroll=4)
    for s in (1, 2, 3):
        my_copy(s).wait_recv()
    top_out[...] = jnp.maximum(jnp.max(myr[...], axis=0), mys[...])
    for i in range(2, 6):
        gb[i].wait_recv()

    for p in (0, 1):
        for c in rs[p]:
            c.wait_send()
        for c in ga[p]:
            c.wait_send()
    for c in gb:
        c.wait_send()
    for d in (sc_drain, t_drain, gq0[2], gq1[2], ret_drain, mx_drain):
        d()
    for s in (1, 2, 3):
        my_copy(s).wait_send()


def writer(npf, mom, rot, top, np_out, nm_out, ns_out, sc_out, scaled, sem):
    first = pltpu.make_async_copy(npf, np_out, sem.at[0])
    second = pltpu.make_async_copy(mom, nm_out, sem.at[1])
    first.start()
    second.start()
    scale = jnp.max(top[...]) + 1e-06
    sc_out[0] = scale
    factor = 31.75 / jnp.broadcast_to(scale, (8, 128))
    wide = jnp.concatenate([factor] * (COLS // 128), axis=1)
    stores = []
    for i in range(NR):

        def step(t, carry, i=i):
            at = pl.ds(pl.multiple_of(t * COLS, 128), COLS)
            scaled[i, :, at] = rot[i, :, at] * wide
            return carry

        lax.fori_loop(0, NF, step, 0, unroll=4)
        stores.append(pltpu.make_async_copy(scaled.at[i], ns_out.at[i], sem.at[2 + i]))
        stores[-1].start()
    for c in [first, second] + stores:
        c.wait()


def body(global_params, local_params, flip_signs, momentum, stale_codes, stale_scale):
    shape = jax.ShapeDtypeStruct
    hbm = pl.BlockSpec(memory_space=pltpu.HBM)
    vmem = pl.BlockSpec(memory_space=pltpu.VMEM)
    smem = pl.BlockSpec(memory_space=pltpu.SMEM)
    dma = pltpu.SemaphoreType.DMA
    w0, w1 = PARTS[0][1], PARTS[1][1]
    col4, row4 = (NF, NR, 8, COLS), (NR, 8, FULL)

    def buf(*dims):
        return pltpu.VMEM(dims, F32)

    results = pl.pallas_call(
        kernel,
        out_shape=(shape(col4, F32), shape(row4, F32), shape(row4, F32), shape((8, 128), F32)),
        in_specs=[hbm, hbm, hbm, hbm, hbm, smem],
        out_specs=(vmem, vmem, vmem, vmem),
        scratch_shapes=[
            buf(*col4), buf(*col4), pltpu.VMEM((FULL // 128, 128), jnp.int32), buf(8, FULL), buf(*row4), buf(*row4),
            pltpu.VMEM((256, 128), BF16),
            buf(2, NF // 2, 8, w0), buf(2, NF // 2, 8, w1), buf(2, NF, 8, w0), buf(2, NF, 8, w1),
            buf(NF, 8, w0), buf(NF, 8, w1), buf(NR, NF, 8, w0), buf(NR, NF, 8, w1),
            buf(NF, 8, w1), buf(NF, 8, w1), buf(NF, NR, 8, w0), buf(NF, NR, 8, w0),
            buf(8, 128), buf(NF, 8, 128), buf(8, 128), buf(3, 8, 128),
            dma((11,)),
            dma((2, 6)), dma((2, 6)), dma((1,)), dma((1,)), dma((1,)), dma((1,)),
            dma((2,)), dma((2,)), dma((2, 6)), dma((2, 6)), dma((6,)), dma((6,)),
            dma((1,)), dma((1,)), dma((1,)), dma((1,)), dma((3,)), dma((3,)),
        ],
        compiler_params=pltpu.CompilerParams(
            collective_id=0, has_side_effects=True, vmem_limit_bytes=43 * 2**20
        ),
        name="outer_step",
    )(
        global_params.reshape(col4), local_params.reshape(col4), flip_signs.reshape(FULL // 128, 128),
        momentum.reshape(row4), stale_codes.reshape(row4), stale_scale,
    )
    new_params, new_momentum, new_stale, new_scale = pl.pallas_call(
        writer,
        out_shape=(shape(col4, F32), shape(row4, F32), shape(row4, F32), shape((1,), F32)),
        in_specs=[vmem] * 4,
        out_specs=(hbm, hbm, hbm, smem),
        scratch_shapes=[buf(*row4), dma((2 + NR,))],
        compiler_params=pltpu.CompilerParams(vmem_limit_bytes=16 * 2**20),
        name="write_results",
    )(*results)
    return (
        new_params.reshape(NF * NR * 8, COLS),
        new_momentum.reshape(NR * 8, FULL),
        new_stale.reshape(NR * 8, FULL),
        new_scale,
    )


def solution(mesh):
    placed = (
        P(None, "fsdp"),
        P("replica", None, "fsdp"),
        P(),
        P("fsdp", None),
        P("fsdp", None),
        P(),
    )
    return jax.shard_map(
        body,
        mesh=mesh,
        in_specs=placed,
        out_specs=(P(None, "fsdp"), P("fsdp", None), P("fsdp", None), P()),
        check_vma=False,
    )
```

time: 129 us -> 110 us (0.85)
  Pallas kernels: 116 us -> 106 us
  local copies, waits for them, and re-layouts: 9.45 us -> 0.89 us
  between operations: 3.07 us -> 1.3 us
    pallas_call x1, Pallas kernels: 116 us -> 102 us  [body(): pl.pallas_call(kernel, out_shape=(shape(col4, F32), shape(row4, F32), sha...]
    unnamed x9 -> x2, local copies, waits for them, and re-layouts: 9.45 us -> 0.89 us
    pallas_call x0 -> x1, Pallas kernels: none -> 4.74 us  [body(): pl.pallas_call(writer, out_shape=(shape(col4, F32), shape(row4, F32), sha...]
where the time goes in v2:
time: 110 us; the launch traced here: 109 us
  Pallas kernels  106 us (96%)
  between operations  1.3 us (1%)
    pallas_call x1, Pallas kernels, body(): pl.pallas_call(kernel, out_shape=(shape(col4, F32), shape(row4, F32), sha...  102 us
    pallas_call x1, Pallas kernels, body(): pl.pallas_call(writer, out_shape=(shape(col4, F32), shape(row4, F32), sha...  4.74 us

profile of v2, /device:TPU:1, one launch (start us, length us, event | category | flops | bytes accessed | tf_op | source)
XLA Modules:
  0.0 108.6 jit_solution(11352879072530358846)
XLA Ops:
  1.3 0.0 copy-start
  1.3 0.9 copy-done
  2.2 101.7 %outer_step.1 = (f32[32,4,8,896]{3,2,1,0:T(8,128)S(1)}, f32[4,8,28672]{2,1,0:T(8,128)S(1)}, f32[4,8,28672]{2,1,0:T(8,128)S(1)}, f32[8,128]{1,0:T(8,128)S(1)}) custom-call(f32[32,4,8,896]{3,2,1,0:T(8,128)} %bitcast.9, f32[32,4,8,896]{3,2,1,0:T(8,128)} %bitcast.10, s32[224,128]{1,0:T(8,128)S(1)} %bitcast.8, f32[4,8,28672]{2,1,0:T(8,128)} %bitcast.11, ...), custom_call_target="tpu_custom_call" | custom-call | tf_op jit(solution)/shard_map/outer_step/pallas_call | solution.py:444
  103.9 4.7 %write_results.1 = (f32[32,4,8,896]{3,2,1,0:T(8,128)}, f32[4,8,28672]{2,1,0:T(8,128)}, f32[4,8,28672]{2,1,0:T(8,128)}, f32[1]{0:T(128)}) custom-call(f32[32,4,8,896]{3,2,1,0:T(8,128)S(1)} %get-tuple-element.12.npf, f32[4,8,28672]{2,1,0:T(8,128)S(1)} %get-tuple-element.13.mom, f32[4,8,28672]{2,1,0:T(8,128)S(1)} %get-tuple-element.14.rot, ...), custom_call_target="tpu_custom_call" | custom-call | tf_op jit(solution)/shard_map/write_results/pallas_call | solution.py:469
Async XLA Ops:
  1.3 0.9 copy-start

commit v3 on v2

--- a/solution.py
+++ b/solution.py
@@ -15,7 +15,7 @@
 BLOCK = 4096
 NBLK = FULL // BLOCK
 PARTS = ((640, 256), (0, 640))
-CUTS = (5, 10)
+CUT = 1
 HALF = (pl.ds(0, NF // 2), pl.ds(NF // 2, NF // 2))
 ORDER = (4, 12, 1, 3, 5, 15, 7, 13, 8, 2, 9, 6, 11, 14, 10)
 PACKED = [sum(v << (4 * i) for i, v in enumerate(ORDER[5 * k : 5 * k + 5])) for k in range(3)]
@@ -32,10 +32,10 @@
 def kernel(
     glob_in, loc_in, flip_in, mom_in, stale_in, sscale_in,
     npf, mom, rot, top_out,
-    glob, pg, signs, flips, stale, xrow, table,
-    r1a, r1b, r2a, r2b, gqa, gqb, gra, grb, tsend, trecv, nsend, nrecv, mxs, mxr, mys, myr,
+    glob, pg, signs, flips, stale, xrow, xpart, table,
+    r1a, r1b, r2a, r2b, gqb, gra, grb, tsend, trecv, nsend, nrecv, mxs, mxr, mys, myr,
     ld_sem,
-    rs_s, rs_r, sc_s, sc_r, t_s, t_r, gq_s, gq_r, ga_s, ga_r, gb_s, gb_r, ret_s, ret_r, mx_s, mx_r, my_s, my_r,
+    rs_s, rs_r, sp_s, sp_r, sc_s, sc_r, t_s, t_r, gq_s, gq_r, ga_s, ga_r, gb_s, gb_r, ret_s, ret_r, mx_s, mx_r, my_s, my_r,
 ):
     r, f = lax.axis_index("replica"), lax.axis_index("fsdp")
     fx, fz, fc = f // 8, lax.rem(f // 2, 4), lax.rem(f, 2)
@@ -130,19 +130,21 @@
 
     r1 = (r1a, r1b)
     r2 = (r2a, r2b)
-    gq = (gqa, gqb)
     gr = (gra, grb)
 
     def cols(p):
         return pl.ds(PARTS[p][0], PARTS[p][1])
+
+    def term(p, half, c):
+        return xpart.at[c, half] if p == 0 else pg.at[half, c, :, cols(1)]
 
     def rs_copies(p):
         lo, hi = HALF
         return (
-            remote(pg.at[lo, far, :, cols(p)], r1[p].at[0], rs_s.at[p, 0], rs_r.at[p, 0], to_right),
-            remote(pg.at[hi, far, :, cols(p)], r1[p].at[1], rs_s.at[p, 1], rs_r.at[p, 1], to_left),
-            remote(pg.at[hi, right, :, cols(p)], r2[p].at[0, hi], rs_s.at[p, 2], rs_r.at[p, 2], to_right),
-            remote(pg.at[lo, left, :, cols(p)], r2[p].at[1, lo], rs_s.at[p, 3], rs_r.at[p, 3], to_left),
+            remote(term(p, lo, far), r1[p].at[0], rs_s.at[p, 0], rs_r.at[p, 0], to_right),
+            remote(term(p, hi, far), r1[p].at[1], rs_s.at[p, 1], rs_r.at[p, 1], to_left),
+            remote(term(p, hi, right), r2[p].at[0, hi], rs_s.at[p, 2], rs_r.at[p, 2], to_right),
+            remote(term(p, lo, left), r2[p].at[1, lo], rs_s.at[p, 3], rs_r.at[p, 3], to_left),
             remote(r1[p].at[0], r2[p].at[0, lo], rs_s.at[p, 4], rs_r.at[p, 4], to_right),
             remote(r1[p].at[1], r2[p].at[1, hi], rs_s.at[p, 5], rs_r.at[p, 5], to_left),
         )
@@ -155,7 +157,7 @@
 
             def add(t, carry, side=side, c=c, base=base):
                 rows = pl.ds(4 * t, 4)
-                r1[p][side, rows] = r1[p][side, rows] + pg[pl.ds(base + 4 * t, 4), c, :, cols(p)]
+                r1[p][side, rows] = r1[p][side, rows] + term(p, pl.ds(base + 4 * t, 4), c)[...]
                 return carry
 
             lax.fori_loop(0, NF // 8, add, 0, unroll=2)
@@ -167,32 +169,37 @@
 
         def add(t, carry):
             rows = pl.ds(4 * t, 4)
-            gq[p][rows] = pg[rows, r, :, cols(p)] + (r2[p][0, rows] + r2[p][1, rows])
+            total = term(p, rows, r)[...] + (r2[p][0, rows] + r2[p][1, rows])
+            if p == 0:
+                gra[r, rows] = total
+            else:
+                gqb[rows] = total
             return carry
 
         lax.fori_loop(0, NF // 4, add, 0, unroll=2)
 
     for i in (0, 1):
-        rs[0][i].start()
+        rs[1][i].start()
     difference(1)
     difference(2)
     for i in (2, 3):
-        rs[0][i].start()
-    for i in (0, 1):
         rs[1][i].start()
     difference(3)
 
+    off1, wid1 = PARTS[1]
+    off0, wid0 = PARTS[0]
+    sp_start, sp_wait, sp_drain = exchange(
+        lambda to: pg.at[to, :, :, cols(0)], lambda frm: xpart.at[:, frm], sp_s.at[0], sp_r.at[0],
+        pg.at[most, :, :, cols(0)], xpart.at[:, most],
+    )
     sc_start, sc_wait, sc_drain = exchange(
-        lambda to: pg.at[to], lambda frm: xrow.at[:, :, lanes(frm)], sc_s.at[0], sc_r.at[0],
-        pg.at[most], xrow.at[:, :, pl.ds(0, (NF - 1) * COLS)],
-    )
-    each_peer(sc_start, 0, CUTS[0], True)
+        lambda to: pg.at[to, :, :, cols(1)], lambda frm: xrow.at[:, :, lanes(frm, wid1, off1)],
+        sc_s.at[0], sc_r.at[0], pg.at[most, :, :, cols(1)], xrow.at[:, :, pl.ds(0, (NF - 1) * wid1)],
+    )
+    each_peer(sp_start)
     for i in range(NR):
-        xrow[i, :, lanes(f)] = pg[f, i]
-
-    rs_second(0)
-    for i in (2, 3):
-        rs[1][i].start()
+        xpart[i, f] = pg[f, i, :, cols(0)]
+        xrow[i, :, lanes(f, wid1, off1)] = pg[f, i, :, cols(1)]
 
     ld_signs.wait()
 
@@ -234,8 +241,6 @@
 
     lax.fori_loop(0, NR * NBLK, stale_step, 0, unroll=4)
     ld_mom.wait()
-    off1, wid1 = PARTS[1]
-    off0, wid0 = PARTS[0]
 
     def t_step(g, carry):
         tsend[g] = 1.9 * stale[r, :, lanes(g, wid1, off1)] + 0.81 * mom[r, :, lanes(g, wid1, off1)]
@@ -249,13 +254,12 @@
     each_peer(t_start)
     trecv[f] = tsend[f]
 
-    def gq_ops(p):
-        return exchange(
-            lambda to: gq[p].at[to], lambda frm: gr[p].at[r, frm], gq_s.at[p], gq_r.at[p],
-            gq[p].at[most], gr[p].at[r, most],
-        )
-
-    gq0, gq1 = gq_ops(0), gq_ops(1)
+    each_peer(sc_start, 0, CUT, True)
+
+    gq_start, gq_wait, gq_drain = exchange(
+        lambda to: gqb.at[to], lambda frm: grb.at[r, frm], gq_s.at[0], gq_r.at[0],
+        gqb.at[most], grb.at[r, most],
+    )
 
     def gather(ref, ss, sr):
         return (
@@ -298,17 +302,21 @@
 
         lax.fori_loop(0, NBLK, rot_step, 0, unroll=NBLK)
 
-    rs_last(0)
-    each_peer(gq0[0])
-    gra[r, f] = gqa[f]
-    each_peer(sc_start, CUTS[0], CUTS[1], False)
     rs_second(1)
-    gq0[1]()
-    gather_start(ga[0])
+    sp_wait()
+    for i in range(4):
+        rs[0][i].start()
+
+    def part_step(t, carry):
+        i, g = t // NF, lax.rem(t, NF)
+        xrow[i, :, lanes(g, wid0, off0)] = xpart[i, g]
+        return carry
+
+    lax.fori_loop(0, NR * NF, part_step, 0, unroll=4)
 
     rs_last(1)
-    each_peer(gq1[0])
-    each_peer(sc_start, CUTS[1], 15, False)
+    each_peer(gq_start)
+    each_peer(sc_start, CUT, 15, False)
     grb[r, f] = gqb[f]
     t_wait()
 
@@ -318,9 +326,15 @@
         return carry
 
     lax.fori_loop(0, NF // 4, np_step, 0, unroll=2)
-    gather_start(gb)
+    rs_second(0)
+    for i in (0, 1):
+        gb[i].start()
+    rs_last(0)
+    gather_start(ga[0])
     gather_forward(ga[0])
-    gq1[1]()
+    for i in (2, 3):
+        gb[i].start()
+    gq_wait()
     gather_start(ga[1])
 
     for i in range(2, 6):
@@ -399,7 +413,7 @@
             c.wait_send()
     for c in gb:
         c.wait_send()
-    for d in (sc_drain, t_drain, gq0[2], gq1[2], ret_drain, mx_drain):
+    for d in (sp_drain, sc_drain, t_drain, gq_drain, ret_drain, mx_drain):
         d()
     for s in (1, 2, 3):
         my_copy(s).wait_send()
@@ -448,14 +462,14 @@
         out_specs=(vmem, vmem, vmem, vmem),
         scratch_shapes=[
             buf(*col4), buf(*col4), pltpu.VMEM((FULL // 128, 128), jnp.int32), buf(8, FULL), buf(*row4), buf(*row4),
-            pltpu.VMEM((256, 128), BF16),
+            buf(NR, NF, 8, w0), pltpu.VMEM((256, 128), BF16),
             buf(2, NF // 2, 8, w0), buf(2, NF // 2, 8, w1), buf(2, NF, 8, w0), buf(2, NF, 8, w1),
-            buf(NF, 8, w0), buf(NF, 8, w1), buf(NR, NF, 8, w0), buf(NR, NF, 8, w1),
+            buf(NF, 8, w1), buf(NR, NF, 8, w0), buf(NR, NF, 8, w1),
             buf(NF, 8, w1), buf(NF, 8, w1), buf(NF, NR, 8, w0), buf(NF, NR, 8, w0),
             buf(8, 128), buf(NF, 8, 128), buf(8, 128), buf(3, 8, 128),
             dma((11,)),
-            dma((2, 6)), dma((2, 6)), dma((1,)), dma((1,)), dma((1,)), dma((1,)),
-            dma((2,)), dma((2,)), dma((2, 6)), dma((2, 6)), dma((6,)), dma((6,)),
+            dma((2, 6)), dma((2, 6)), dma((1,)), dma((1,)), dma((1,)), dma((1,)), dma((1,)), dma((1,)),
+            dma((1,)), dma((1,)), dma((2, 6)), dma((2, 6)), dma((6,)), dma((6,)),
             dma((1,)), dma((1,)), dma((1,)), dma((1,)), dma((3,)), dma((3,)),
         ],
         compiler_params=pltpu.CompilerParams(

time: 110 us -> 99.5 us (0.905); the launches traced: 109 us -> 99.4 us
  Pallas kernels: 106 us -> 97.2 us
    pallas_call x1, Pallas kernels: 102 us -> 92.4 us  [body(): pl.pallas_call(kernel, out_shape=(shape(col4, F32), shape(row4, F32), sha...]
where the time goes in v3:
time: 99.5 us; the launch traced here: 99.4 us
  Pallas kernels  97.2 us (98%)
  between operations  1.3 us (1%)
    pallas_call x1, Pallas kernels, body(): pl.pallas_call(kernel, out_shape=(shape(col4, F32), shape(row4, F32), sha...  92.4 us
    pallas_call x1, Pallas kernels, body(): pl.pallas_call(writer, out_shape=(shape(col4, F32), shape(row4, F32), sha...  4.74 us

profile of v3, /device:TPU:1, one launch (start us, length us, event | category | flops | bytes accessed | tf_op | source)
XLA Modules:
  0.0 99.4 jit_solution(16004929633654869393)
XLA Ops:
  1.3 0.0 copy-start
  1.3 0.9 copy-done
  2.2 92.4 %outer_step.1 = (f32[32,4,8,896]{3,2,1,0:T(8,128)S(1)}, f32[4,8,28672]{2,1,0:T(8,128)S(1)}, f32[4,8,28672]{2,1,0:T(8,128)S(1)}, f32[8,128]{1,0:T(8,128)S(1)}) custom-call(f32[32,4,8,896]{3,2,1,0:T(8,128)} %bitcast.9, f32[32,4,8,896]{3,2,1,0:T(8,128)} %bitcast.10, s32[224,128]{1,0:T(8,128)S(1)} %bitcast.8, f32[4,8,28672]{2,1,0:T(8,128)} %bitcast.11, ...), custom_call_target="tpu_custom_call" | custom-call | tf_op jit(solution)/shard_map/outer_step/pallas_call | solution.py:458
  94.6 4.7 %write_results.1 = (f32[32,4,8,896]{3,2,1,0:T(8,128)}, f32[4,8,28672]{2,1,0:T(8,128)}, f32[4,8,28672]{2,1,0:T(8,128)}, f32[1]{0:T(128)}) custom-call(f32[32,4,8,896]{3,2,1,0:T(8,128)S(1)} %get-tuple-element.12.npf, f32[4,8,28672]{2,1,0:T(8,128)S(1)} %get-tuple-element.13.mom, f32[4,8,28672]{2,1,0:T(8,128)S(1)} %get-tuple-element.14.rot, ...), custom_call_target="tpu_custom_call" | custom-call | tf_op jit(solution)/shard_map/write_results/pallas_call | solution.py:483
Async XLA Ops:
  1.3 0.9 copy-start

commit v4 on v3

--- a/solution.py
+++ b/solution.py
@@ -14,7 +14,7 @@
 FULL = NF * COLS
 BLOCK = 4096
 NBLK = FULL // BLOCK
-PARTS = ((640, 256), (0, 640))
+PARTS = ((512, 384), (0, 512))
 CUT = 1
 HALF = (pl.ds(0, NF // 2), pl.ds(NF // 2, NF // 2))
 ORDER = (4, 12, 1, 3, 5, 15, 7, 13, 8, 2, 9, 6, 11, 14, 10)
@@ -86,22 +86,22 @@
 
     most = pl.ds(0, NF - 1)
 
-    order = (far, right, left, r)
+    order = ((far, 2), (left, 3), (right, 1), (r, 0))
     loads = []
-    for i, c in enumerate(order):
-        a = pltpu.make_async_copy(loc_in.at[:, c], pg.at[:, c], ld_sem.at[2 * i])
+    for i, (c, j) in enumerate(order):
+        a = pltpu.make_async_copy(loc_in.at[:, c], pg.at[:, j], ld_sem.at[2 * i])
         b = pltpu.make_async_copy(glob_in.at[:, c], glob.at[:, c], ld_sem.at[2 * i + 1])
-        a.start()
-        b.start()
         loads.append((a, b))
     ld_stale = pltpu.make_async_copy(stale_in, stale, ld_sem.at[8])
     ld_mom = pltpu.make_async_copy(mom_in, mom, ld_sem.at[9])
     ld_signs = pltpu.make_async_copy(flip_in, signs, ld_sem.at[10])
-    ld_signs.start()
-    ld_stale.start()
-    ld_mom.start()
+    for load in loads[0]:
+        load.start()
 
     barrier = pltpu.get_barrier_semaphore()
+
+    for s in (1, 2, 3):
+        pl.semaphore_signal(barrier, inc=1, device_id=(lax.rem(r + s, 4), f), device_id_type=MESH)
 
     def greet(s, carry):
         pl.semaphore_signal(
@@ -110,21 +110,22 @@
         return carry
 
     lax.fori_loop(1, NF, greet, 0)
-    for s in (1, 2, 3):
-        pl.semaphore_signal(barrier, inc=1, device_id=(lax.rem(r + s, 4), f), device_id_type=MESH)
 
     def difference(i):
-        c = order[i]
+        c, j = order[i]
         for load in loads[i]:
             load.wait()
 
         def diff(t, carry):
             rows = pl.ds(4 * t, 4)
-            pg[rows, c] = glob[rows, c] - pg[rows, c]
+            pg[rows, j] = glob[rows, c] - pg[rows, j]
             return carry
 
         lax.fori_loop(0, NF // 4, diff, 0, unroll=2)
 
+    for i in (1, 2, 3):
+        for load in loads[i]:
+            load.start()
     difference(0)
     pl.semaphore_wait(barrier, NF - 1 + NR - 1)
 
@@ -135,16 +136,16 @@
     def cols(p):
         return pl.ds(PARTS[p][0], PARTS[p][1])
 
-    def term(p, half, c):
-        return xpart.at[c, half] if p == 0 else pg.at[half, c, :, cols(1)]
+    def term(p, half, j):
+        return xpart.at[j, half] if p == 0 else pg.at[half, j, :, cols(1)]
 
     def rs_copies(p):
         lo, hi = HALF
         return (
-            remote(term(p, lo, far), r1[p].at[0], rs_s.at[p, 0], rs_r.at[p, 0], to_right),
-            remote(term(p, hi, far), r1[p].at[1], rs_s.at[p, 1], rs_r.at[p, 1], to_left),
-            remote(term(p, hi, right), r2[p].at[0, hi], rs_s.at[p, 2], rs_r.at[p, 2], to_right),
-            remote(term(p, lo, left), r2[p].at[1, lo], rs_s.at[p, 3], rs_r.at[p, 3], to_left),
+            remote(term(p, lo, 2), r1[p].at[0], rs_s.at[p, 0], rs_r.at[p, 0], to_right),
+            remote(term(p, hi, 2), r1[p].at[1], rs_s.at[p, 1], rs_r.at[p, 1], to_left),
+            remote(term(p, hi, 1), r2[p].at[0, hi], rs_s.at[p, 2], rs_r.at[p, 2], to_right),
+            remote(term(p, lo, 3), r2[p].at[1, lo], rs_s.at[p, 3], rs_r.at[p, 3], to_left),
             remote(r1[p].at[0], r2[p].at[0, lo], rs_s.at[p, 4], rs_r.at[p, 4], to_right),
             remote(r1[p].at[1], r2[p].at[1, hi], rs_s.at[p, 5], rs_r.at[p, 5], to_left),
         )
@@ -152,12 +153,12 @@
     rs = (rs_copies(0), rs_copies(1))
 
     def rs_second(p):
-        for side, c, base in ((0, right, 0), (1, left, NF // 2)):
+        for side, j, base in ((0, 1, 0), (1, 3, NF // 2)):
             rs[p][side].wait_recv()
 
-            def add(t, carry, side=side, c=c, base=base):
+            def add(t, carry, side=side, j=j, base=base):
                 rows = pl.ds(4 * t, 4)
-                r1[p][side, rows] = r1[p][side, rows] + term(p, pl.ds(base + 4 * t, 4), c)[...]
+                r1[p][side, rows] = r1[p][side, rows] + term(p, pl.ds(base + 4 * t, 4), j)[...]
                 return carry
 
             lax.fori_loop(0, NF // 8, add, 0, unroll=2)
@@ -169,7 +170,7 @@
 
         def add(t, carry):
             rows = pl.ds(4 * t, 4)
-            total = term(p, rows, r)[...] + (r2[p][0, rows] + r2[p][1, rows])
+            total = term(p, rows, 0)[...] + (r2[p][0, rows] + r2[p][1, rows])
             if p == 0:
                 gra[r, rows] = total
             else:
@@ -180,23 +181,31 @@
 
     for i in (0, 1):
         rs[1][i].start()
+    ld_signs.start()
+    ld_stale.start()
+    ld_mom.start()
     difference(1)
     difference(2)
-    for i in (2, 3):
+    for i in (3, 2):
         rs[1][i].start()
     difference(3)
 
     off1, wid1 = PARTS[1]
     off0, wid0 = PARTS[0]
-    sp_start, sp_wait, sp_drain = exchange(
-        lambda to: pg.at[to, :, :, cols(0)], lambda frm: xpart.at[:, frm], sp_s.at[0], sp_r.at[0],
-        pg.at[most, :, :, cols(0)], xpart.at[:, most],
-    )
+    def sp_exchange(k):
+        pair = pl.ds(2 * k, 2)
+        return exchange(
+            lambda to: pg.at[to, pair, :, cols(0)], lambda frm: xpart.at[pair, frm],
+            sp_s.at[k], sp_r.at[k], pg.at[most, pair, :, cols(0)], xpart.at[pair, most],
+        )
+
+    sp = (sp_exchange(0), sp_exchange(1))
     sc_start, sc_wait, sc_drain = exchange(
         lambda to: pg.at[to, :, :, cols(1)], lambda frm: xrow.at[:, :, lanes(frm, wid1, off1)],
         sc_s.at[0], sc_r.at[0], pg.at[most, :, :, cols(1)], xrow.at[:, :, pl.ds(0, (NF - 1) * wid1)],
     )
-    each_peer(sp_start)
+    each_peer(sp[1][0])
+    each_peer(sp[0][0])
     for i in range(NR):
         xpart[i, f] = pg[f, i, :, cols(0)]
         xrow[i, :, lanes(f, wid1, off1)] = pg[f, i, :, cols(1)]
@@ -303,9 +312,11 @@
         lax.fori_loop(0, NBLK, rot_step, 0, unroll=NBLK)
 
     rs_second(1)
-    sp_wait()
-    for i in range(4):
+    sp[1][1]()
+    for i in (0, 1, 3):
         rs[0][i].start()
+    sp[0][1]()
+    rs[0][2].start()
 
     def part_step(t, carry):
         i, g = t // NF, lax.rem(t, NF)
@@ -353,13 +364,10 @@
         lambda to: nsend.at[to], lambda frm: nrecv.at[frm], ret_s.at[0], ret_r.at[0],
         nsend.at[most], nrecv.at[most],
     )
-    each_peer(ret_start)
+    each_peer(ret_start, 0, 6, False)
     nrecv[f] = nsend[f]
 
     rows_of(r)
-    gather_forward(ga[1])
-    gather_forward(gb)
-
     sc_wait()
 
     def scale_step(t, top):
@@ -372,7 +380,11 @@
         lambda to: mxs, lambda frm: mxr.at[frm], mx_s.at[0], mx_r.at[0], mxr.at[most], mxr.at[most]
     )
     each_peer(mx_start)
+    each_peer(ret_start, 6, 15, True)
     mxr[f] = mxs[...]
+
+    gather_forward(ga[1])
+    gather_forward(gb)
 
     ga[1][3].wait_recv()
     rows_of(right)
@@ -413,22 +425,24 @@
             c.wait_send()
     for c in gb:
         c.wait_send()
-    for d in (sp_drain, sc_drain, t_drain, gq_drain, ret_drain, mx_drain):
+    for d in (sp[0][2], sp[1][2], sc_drain, t_drain, gq_drain, ret_drain, mx_drain):
         d()
     for s in (1, 2, 3):
         my_copy(s).wait_send()
 
 
 def writer(npf, mom, rot, top, np_out, nm_out, ns_out, sc_out, scaled, sem):
-    first = pltpu.make_async_copy(npf, np_out, sem.at[0])
-    second = pltpu.make_async_copy(mom, nm_out, sem.at[1])
-    first.start()
-    second.start()
+    stores = []
+    for i in range(NR):
+        rows = pl.ds(8 * i, 8)
+        stores.append(pltpu.make_async_copy(npf.at[rows], np_out.at[rows], sem.at[i]))
+        stores.append(pltpu.make_async_copy(mom.at[i], nm_out.at[i], sem.at[4 + i]))
+    for c in stores:
+        c.start()
     scale = jnp.max(top[...]) + 1e-06
     sc_out[0] = scale
     factor = 31.75 / jnp.broadcast_to(scale, (8, 128))
     wide = jnp.concatenate([factor] * (COLS // 128), axis=1)
-    stores = []
     for i in range(NR):
 
         def step(t, carry, i=i):
@@ -437,9 +451,9 @@
             return carry
 
         lax.fori_loop(0, NF, step, 0, unroll=4)
-        stores.append(pltpu.make_async_copy(scaled.at[i], ns_out.at[i], sem.at[2 + i]))
+        stores.append(pltpu.make_async_copy(scaled.at[i], ns_out.at[i], sem.at[8 + i]))
         stores[-1].start()
-    for c in [first, second] + stores:
+    for c in stores:
         c.wait()
 
 
@@ -468,7 +482,7 @@
             buf(NF, 8, w1), buf(NF, 8, w1), buf(NF, NR, 8, w0), buf(NF, NR, 8, w0),
             buf(8, 128), buf(NF, 8, 128), buf(8, 128), buf(3, 8, 128),
             dma((11,)),
-            dma((2, 6)), dma((2, 6)), dma((1,)), dma((1,)), dma((1,)), dma((1,)), dma((1,)), dma((1,)),
+            dma((2, 6)), dma((2, 6)), dma((2,)), dma((2,)), dma((1,)), dma((1,)), dma((1,)), dma((1,)),
             dma((1,)), dma((1,)), dma((2, 6)), dma((2, 6)), dma((6,)), dma((6,)),
             dma((1,)), dma((1,)), dma((1,)), dma((1,)), dma((3,)), dma((3,)),
         ],
@@ -485,7 +499,7 @@
         out_shape=(shape(col4, F32), shape(row4, F32), shape(row4, F32), shape((1,), F32)),
         in_specs=[vmem] * 4,
         out_specs=(hbm, hbm, hbm, smem),
-        scratch_shapes=[buf(*row4), dma((2 + NR,))],
+        scratch_shapes=[buf(*row4), dma((3 * NR,))],
         compiler_params=pltpu.CompilerParams(vmem_limit_bytes=16 * 2**20),
         name="write_results",
     )(*results)

time: 99.5 us -> 97 us (0.975)
  Pallas kernels: 97.2 us -> 94.7 us
    pallas_call x1, Pallas kernels: 92.4 us -> 90 us  [body(): pl.pallas_call(kernel, out_shape=(shape(col4, F32), shape(row4, F32), sha...]
where the time goes in v4:
time: 97 us; the launch traced here: 96.9 us
  Pallas kernels  94.7 us (98%)
  between operations  1.3 us (1%)
    pallas_call x1, Pallas kernels, body(): pl.pallas_call(kernel, out_shape=(shape(col4, F32), shape(row4, F32), sha...  90 us
    pallas_call x1, Pallas kernels, body(): pl.pallas_call(writer, out_shape=(shape(col4, F32), shape(row4, F32), sha...  4.71 us

profile of v4, /device:TPU:1, one launch (start us, length us, event | category | flops | bytes accessed | tf_op | source)
XLA Modules:
  0.0 96.9 jit_solution(16269030997300917291)
XLA Ops:
  1.3 0.0 copy-start
  1.3 0.9 copy-done
  2.2 90.0 %outer_step.1 = (f32[32,4,8,896]{3,2,1,0:T(8,128)S(1)}, f32[4,8,28672]{2,1,0:T(8,128)S(1)}, f32[4,8,28672]{2,1,0:T(8,128)S(1)}, f32[8,128]{1,0:T(8,128)S(1)}) custom-call(f32[32,4,8,896]{3,2,1,0:T(8,128)} %bitcast.9, f32[32,4,8,896]{3,2,1,0:T(8,128)} %bitcast.10, s32[224,128]{1,0:T(8,128)S(1)} %bitcast.8, f32[4,8,28672]{2,1,0:T(8,128)} %bitcast.11, ...), custom_call_target="tpu_custom_call" | custom-call | tf_op jit(solution)/shard_map/outer_step/pallas_call | solution.py:472
  92.1 4.7 %write_results.1 = (f32[32,4,8,896]{3,2,1,0:T(8,128)}, f32[4,8,28672]{2,1,0:T(8,128)}, f32[4,8,28672]{2,1,0:T(8,128)}, f32[1]{0:T(128)}) custom-call(f32[32,4,8,896]{3,2,1,0:T(8,128)S(1)} %get-tuple-element.12.npf, f32[4,8,28672]{2,1,0:T(8,128)S(1)} %get-tuple-element.13.mom, f32[4,8,28672]{2,1,0:T(8,128)S(1)} %get-tuple-element.14.rot, ...), custom_call_target="tpu_custom_call" | custom-call | tf_op jit(solution)/shard_map/write_results/pallas_call | solution.py:497
Async XLA Ops:
  1.3 0.9 copy-start

commit v5 on v4

--- a/solution.py
+++ b/solution.py
@@ -181,15 +181,6 @@
 
     for i in (0, 1):
         rs[1][i].start()
-    ld_signs.start()
-    ld_stale.start()
-    ld_mom.start()
-    difference(1)
-    difference(2)
-    for i in (3, 2):
-        rs[1][i].start()
-    difference(3)
-
     off1, wid1 = PARTS[1]
     off0, wid0 = PARTS[0]
     def sp_exchange(k):
@@ -204,7 +195,15 @@
         lambda to: pg.at[to, :, :, cols(1)], lambda frm: xrow.at[:, :, lanes(frm, wid1, off1)],
         sc_s.at[0], sc_r.at[0], pg.at[most, :, :, cols(1)], xrow.at[:, :, pl.ds(0, (NF - 1) * wid1)],
     )
+    difference(1)
+    rs[1][3].start()
     each_peer(sp[1][0])
+    ld_signs.start()
+    ld_stale.start()
+    ld_mom.start()
+    difference(2)
+    rs[1][2].start()
+    difference(3)
     each_peer(sp[0][0])
     for i in range(NR):
         xpart[i, f] = pg[f, i, :, cols(0)]
@@ -364,7 +363,7 @@
         lambda to: nsend.at[to], lambda frm: nrecv.at[frm], ret_s.at[0], ret_r.at[0],
         nsend.at[most], nrecv.at[most],
     )
-    each_peer(ret_start, 0, 6, False)
+    each_peer(ret_start, 0, 9, False)
     nrecv[f] = nsend[f]
 
     rows_of(r)
@@ -380,7 +379,7 @@
         lambda to: mxs, lambda frm: mxr.at[frm], mx_s.at[0], mx_r.at[0], mxr.at[most], mxr.at[most]
     )
     each_peer(mx_start)
-    each_peer(ret_start, 6, 15, True)
+    each_peer(ret_start, 9, 15, True)
     mxr[f] = mxs[...]
 
     gather_forward(ga[1])
@@ -390,20 +389,20 @@
     rows_of(right)
     ga[1][2].wait_recv()
     rows_of(left)
+    mx_wait()
+    mys[...] = jnp.max(mxr[...], axis=0)
+
+    def my_copy(s):
+        return remote(
+            mys, myr.at[s - 1], my_s.at[s - 1], my_r.at[s - 1], (lax.rem(r + s, 4), f)
+        )
+
+    for s in (1, 2, 3):
+        my_copy(s).start()
+
     for i in (4, 5):
         ga[1][i].wait_recv()
     rows_of(far)
-
-    mx_wait()
-    mys[...] = jnp.max(mxr[...], axis=0)
-
-    def my_copy(s):
-        return remote(
-            mys, myr.at[s - 1], my_s.at[s - 1], my_r.at[s - 1], (lax.rem(r + s, 4), f)
-        )
-
-    for s in (1, 2, 3):
-        my_copy(s).start()
 
     ret_wait()
 

time: 97 us -> 96.1 us (level)
  no operation moved by 1% of the time
where the time goes in v5:
time: 96.1 us; the launch traced here: 96 us
  Pallas kernels  93.8 us (98%)
  between operations  1.3 us (1%)
    pallas_call x1, Pallas kernels, body(): pl.pallas_call(kernel, out_shape=(shape(col4, F32), shape(row4, F32), sha...  89.1 us
    pallas_call x1, Pallas kernels, body(): pl.pallas_call(writer, out_shape=(shape(col4, F32), shape(row4, F32), sha...  4.71 us

profile of v5, /device:TPU:1, one launch (start us, length us, event | category | flops | bytes accessed | tf_op | source)
XLA Modules:
  0.0 96.0 jit_solution(7250357930335898699)
XLA Ops:
  1.3 0.0 copy-start
  1.3 0.9 copy-done
  2.2 89.1 %outer_step.1 = (f32[32,4,8,896]{3,2,1,0:T(8,128)S(1)}, f32[4,8,28672]{2,1,0:T(8,128)S(1)}, f32[4,8,28672]{2,1,0:T(8,128)S(1)}, f32[8,128]{1,0:T(8,128)S(1)}) custom-call(f32[32,4,8,896]{3,2,1,0:T(8,128)} %bitcast.9, f32[32,4,8,896]{3,2,1,0:T(8,128)} %bitcast.10, s32[224,128]{1,0:T(8,128)S(1)} %bitcast.8, f32[4,8,28672]{2,1,0:T(8,128)} %bitcast.11, ...), custom_call_target="tpu_custom_call" | custom-call | tf_op jit(solution)/shard_map/outer_step/pallas_call | solution.py:471
  91.3 4.7 %write_results.1 = (f32[32,4,8,896]{3,2,1,0:T(8,128)}, f32[4,8,28672]{2,1,0:T(8,128)}, f32[4,8,28672]{2,1,0:T(8,128)}, f32[1]{0:T(128)}) custom-call(f32[32,4,8,896]{3,2,1,0:T(8,128)S(1)} %get-tuple-element.12.npf, f32[4,8,28672]{2,1,0:T(8,128)S(1)} %get-tuple-element.13.mom, f32[4,8,28672]{2,1,0:T(8,128)S(1)} %get-tuple-element.14.rot, ...), custom_call_target="tpu_custom_call" | custom-call | tf_op jit(solution)/shard_map/write_results/pallas_call | solution.py:496
Async XLA Ops:
  1.3 0.9 copy-start

commit v6 on v5

--- a/solution.py
+++ b/solution.py
@@ -123,10 +123,12 @@
 
         lax.fori_loop(0, NF // 4, diff, 0, unroll=2)
 
-    for i in (1, 2, 3):
+    for load in loads[1]:
+        load.start()
+    difference(0)
+    for i in (2, 3):
         for load in loads[i]:
             load.start()
-    difference(0)
     pl.semaphore_wait(barrier, NF - 1 + NR - 1)
 
     r1 = (r1a, r1b)

time: 96.1 us -> 96.1 us (level)
  no operation moved by 1% of the time
where the time goes in v6:
time: 96.1 us; the launch traced here: 96 us
  Pallas kernels  93.8 us (98%)
  between operations  1.3 us (1%)
    pallas_call x1, Pallas kernels, body(): pl.pallas_call(kernel, out_shape=(shape(col4, F32), shape(row4, F32), sha...  89.1 us
    pallas_call x1, Pallas kernels, body(): pl.pallas_call(writer, out_shape=(shape(col4, F32), shape(row4, F32), sha...  4.71 us

profile of v6, /device:TPU:1, one launch (start us, length us, event | category | flops | bytes accessed | tf_op | source)
XLA Modules:
  0.0 96.0 jit_solution(17162770267491348918)
XLA Ops:
  1.3 0.0 copy-start
  1.3 0.9 copy-done
  2.2 89.1 %outer_step.1 = (f32[32,4,8,896]{3,2,1,0:T(8,128)S(1)}, f32[4,8,28672]{2,1,0:T(8,128)S(1)}, f32[4,8,28672]{2,1,0:T(8,128)S(1)}, f32[8,128]{1,0:T(8,128)S(1)}) custom-call(f32[32,4,8,896]{3,2,1,0:T(8,128)} %bitcast.9, f32[32,4,8,896]{3,2,1,0:T(8,128)} %bitcast.10, s32[224,128]{1,0:T(8,128)S(1)} %bitcast.8, f32[4,8,28672]{2,1,0:T(8,128)} %bitcast.11, ...), custom_call_target="tpu_custom_call" | custom-call | tf_op jit(solution)/shard_map/outer_step/pallas_call | solution.py:473
  91.3 4.7 %write_results.1 = (f32[32,4,8,896]{3,2,1,0:T(8,128)}, f32[4,8,28672]{2,1,0:T(8,128)}, f32[4,8,28672]{2,1,0:T(8,128)}, f32[1]{0:T(128)}) custom-call(f32[32,4,8,896]{3,2,1,0:T(8,128)S(1)} %get-tuple-element.12.npf, f32[4,8,28672]{2,1,0:T(8,128)S(1)} %get-tuple-element.13.mom, f32[4,8,28672]{2,1,0:T(8,128)S(1)} %get-tuple-element.14.rot, ...), custom_call_target="tpu_custom_call" | custom-call | tf_op jit(solution)/shard_map/write_results/pallas_call | solution.py:498
Async XLA Ops:
  1.3 0.9 copy-start
